TPU v7x, 256 devices: a whole 4x4x8 slice. The times are simulated.
256 devices in a mesh: seq: 32 (over z_lo, x, y), head: 8 (over z_hi, core).
Axes of the slice: x: 4, y: 4, z: 8 (z_hi: 4, z_lo: 2; z = z_hi * 2 + z_lo), core: 2. Of those that a mesh axis runs over, the one named last changes fastest.
Arguments:
- query_tokens: bfloat16 [40960, 3072], P(('seq', 'head')), may hold values from -6 to 6
- key_tokens: bfloat16 [40960, 3072], P(('seq', 'head')), may hold values from -6 to 6
- value_tokens: bfloat16 [40960, 3072], P(('seq', 'head')), may hold values from -6 to 6
- matching: int32 [2, 32], replicated, may hold values from 0 to 31, as said below
Outputs:
- attended: bfloat16 [40960, 3072], P(('seq', 'head'))
Inputs may be any that keep to these rules, and one draw needn't show every extreme that they name: For each round r and block b: matching[r, matching[r, b]] == b and matching[r, b] != b; the 2 rows give every block different partners.
All inputs are finite; a program needn't handle non-finite values.
Results may differ from a plain program's by a relative error of at most 0.0048.
Values may be sent and summed in bfloat16 or wider, within the bound.
A program may use at most 64 MiB of HBM per device.

v0:
```python
import math

import jax
import jax.numpy as jnp
from jax import lax
from jax.sharding import PartitionSpec as P

HEAD_DIM = 128
ROUNDS = 2


def attend(query_rows, key_rows, value_rows, head_size):
    row_count, feature_width = query_rows.shape
    heads_here = feature_width // head_size
    block_rows = math.gcd(row_count, 512)
    score_scale = 1.0 / math.sqrt(head_size)
    key_heads = key_rows.reshape(-1, heads_here, head_size)
    value_heads = value_rows.reshape(-1, heads_here, head_size)
    query_blocks = query_rows.reshape(row_count // block_rows, block_rows, heads_here, head_size)

    def one_block(query_block):
        scores = (
            jnp.einsum("qhd,khd->hqk", query_block, key_heads, preferred_element_type=jnp.float32)
            * score_scale
        )
        weights = jnp.exp(scores - jnp.max(scores, axis=-1, keepdims=True))
        totals = jnp.sum(weights, axis=-1)
        mixed = jnp.einsum(
            "hqk,khd->qhd",
            weights.astype(jnp.bfloat16),
            value_heads,
            preferred_element_type=jnp.float32,
        )
        return (mixed / jnp.transpose(totals)[:, :, None]).astype(jnp.bfloat16)

    return lax.map(one_block, query_blocks).reshape(row_count, feature_width)


def per_device(query_tokens, key_tokens, value_tokens, matching):
    seq_count = lax.axis_size("seq")
    local_query, local_keys, local_values = (
        lax.all_to_all(query_tokens, "head", split_axis=1, concat_axis=0, tiled=True),
        lax.all_to_all(key_tokens, "head", split_axis=1, concat_axis=0, tiled=True),
        lax.all_to_all(value_tokens, "head", split_axis=1, concat_axis=0, tiled=True),
    )
    block_count, feature_width = local_keys.shape
    piece_rows = block_count // seq_count
    spread_keys, spread_values = (
        lax.all_to_all(
            local_keys.reshape(seq_count, piece_rows, feature_width),
            "seq",
            split_axis=0,
            concat_axis=0,
            tiled=True,
        ),
        lax.all_to_all(
            local_values.reshape(seq_count, piece_rows, feature_width),
            "seq",
            split_axis=0,
            concat_axis=0,
            tiled=True,
        ),
    )
    key_parts = []
    value_parts = []
    for round_index in range(ROUNDS):
        got_keys, got_values = (
            lax.all_to_all(
                jnp.take(spread_keys, matching[round_index], axis=0),
                "seq",
                split_axis=0,
                concat_axis=0,
                tiled=True,
            ),
            lax.all_to_all(
                jnp.take(spread_values, matching[round_index], axis=0),
                "seq",
                split_axis=0,
                concat_axis=0,
                tiled=True,
            ),
        )
        key_parts.append(got_keys.reshape(block_count, feature_width))
        value_parts.append(got_values.reshape(block_count, feature_width))
    partner_keys = jnp.concatenate(key_parts, 0)
    partner_values = jnp.concatenate(value_parts, 0)
    key_rows = jnp.concatenate([local_keys, partner_keys], 0)
    value_rows = jnp.concatenate([local_values, partner_values], 0)
    attended = attend(local_query, key_rows, value_rows, HEAD_DIM)
    return lax.all_to_all(attended, "head", split_axis=0, concat_axis=1, tiled=True)


def solution(mesh):
    return jax.shard_map(
        per_device,
        mesh=mesh,
        in_specs=(
            P(("seq", "head"), None),
            P(("seq", "head"), None),
            P(("seq", "head"), None),
            P(),
        ),
        out_specs=P(("seq", "head"), None),
        check_vma=False,
    )
```

profile of v0, /device:TPU:1, one launch (start us, length us, event | category | flops | bytes accessed | tf_op | source)
XLA Modules:
  0.0 338.2 jit_solution(16645471671025664687)
XLA Ops:
  2.3 10.0 %all-to-all-start.1 = ((bf16[160,8,384]{2,0,1:T(8,128)(2,1)}), bf16[160,8,384]{2,0,1:T(8,128)(2,1)S(1)}, u32[]{:S(2)}, u32[]{:S(2)}) async-start(bf16[160,8,384]{2,0,1:T(8,128)(2,1)} %bitcast.48), calls=%async_computation.1 | async-start | bytes 1966080 | tf_op jit(solution)/shard_map/all_to_all | solution.py:43
  12.4 22.9 %all-to-all-done.1 = bf16[160,8,384]{2,0,1:T(8,128)(2,1)S(1)} async-done(((bf16[160,8,384]{2,0,1:T(8,128)(2,1)}), bf16[160,8,384]{2,0,1:T(8,128)(2,1)S(1)}, u32[]{:S(2)}, u32[]{:S(2)}) %all-to-all-start.1) | async-done | bytes 983072 | tf_op jit(solution)/shard_map/all_to_all | solution.py:43
  35.3 32.4 %all_to_all.97 = bf16[160,8,384]{2,0,1:T(8,128)(2,1)} all-to-all(bf16[160,8,384]{2,0,1:T(8,128)(2,1)S(1)} %bitcast.65), channel_id=1, replica_groups=mesh['seq'=32,'head'=8] {'head'}, dimensions={1} | all-to-all | bytes 1966080 | tf_op jit(solution)/shard_map/all_to_all | solution.py:44
  67.7 21.4 %all_to_all.98 = bf16[32,40,384]{2,1,0:T(8,128)(2,1)S(1)} all-to-all(bf16[32,40,384]{2,1,0:T(8,128)(2,1)S(1)} %bitcast.62), channel_id=1, replica_groups=mesh['seq'=32,'head'=8] {'seq'}, dimensions={0} | all-to-all | bytes 1966080 | tf_op jit(solution)/shard_map/all_to_all | solution.py:49
  89.2 5.2 %all-to-all-start.6 = ((bf16[32,40,384]{2,1,0:T(8,128)(2,1)}), bf16[32,40,384]{2,1,0:T(8,128)(2,1)S(1)}, u32[]{:S(2)}, u32[]{:S(2)}) async-start(bf16[32,40,384]{2,1,0:T(8,128)(2,1)} %bitcast.10), calls=%async_computation.6 | async-start | bytes 1966080 | tf_op jit(solution)/shard_map/all_to_all | solution.py:56
  96.6 9.3 %all-to-all-done.6 = bf16[32,40,384]{2,1,0:T(8,128)(2,1)S(1)} async-done(((bf16[32,40,384]{2,1,0:T(8,128)(2,1)}), bf16[32,40,384]{2,1,0:T(8,128)(2,1)S(1)}, u32[]{:S(2)}, u32[]{:S(2)}) %all-to-all-start.6) | async-done | bytes 983072 | tf_op jit(solution)/shard_map/all_to_all | solution.py:56
  106.0 9.7 %all-to-all-start = ((bf16[160,8,384]{2,0,1:T(8,128)(2,1)}), bf16[160,8,384]{2,0,1:T(8,128)(2,1)}, u32[]{:S(2)}, u32[]{:S(2)}) async-start(bf16[160,8,384]{2,0,1:T(8,128)(2,1)} %bitcast.64), calls=%async_computation | async-start | bytes 1966080 | tf_op jit(solution)/shard_map/all_to_all | solution.py:42
  122.1 14.1 %all-to-all-done = bf16[160,8,384]{2,0,1:T(8,128)(2,1)} async-done(((bf16[160,8,384]{2,0,1:T(8,128)(2,1)}), bf16[160,8,384]{2,0,1:T(8,128)(2,1)}, u32[]{:S(2)}, u32[]{:S(2)}) %all-to-all-start) | async-done | bytes 983072 | tf_op jit(solution)/shard_map/all_to_all | solution.py:42
  136.3 11.3 %all-to-all-start.3 = ((bf16[32,40,384]{2,1,0:T(8,128)(2,1)}), bf16[32,40,384]{2,1,0:T(8,128)(2,1)}, u32[]{:S(2)}, u32[]{:S(2)}) async-start(bf16[32,40,384]{2,1,0:T(8,128)(2,1)} %get-tuple-element.68), calls=%async_computation.3 | async-start | bytes 1966080 | tf_op jit(solution)/shard_map/all_to_all | solution.py:68
  153.7 7.8 %all-to-all-done.3 = bf16[32,40,384]{2,1,0:T(8,128)(2,1)} async-done(((bf16[32,40,384]{2,1,0:T(8,128)(2,1)}), bf16[32,40,384]{2,1,0:T(8,128)(2,1)}, u32[]{:S(2)}, u32[]{:S(2)}) %all-to-all-start.3) | async-done | bytes 983072 | tf_op jit(solution)/shard_map/all_to_all | solution.py:68
  161.5 18.8 %all_to_all.99 = bf16[32,40,384]{2,1,0:T(8,128)(2,1)} all-to-all(bf16[32,40,384]{2,1,0:T(8,128)(2,1)S(1)} %get-tuple-element.70), channel_id=1, replica_groups=mesh['seq'=32,'head'=8] {'seq'}, dimensions={0} | all-to-all | bytes 1966080 | tf_op jit(solution)/shard_map/all_to_all | solution.py:68
  180.3 16.9 %all_to_all.100 = bf16[32,40,384]{2,1,0:T(8,128)(2,1)} all-to-all(bf16[32,40,384]{2,1,0:T(8,128)(2,1)S(1)} %copy-done), channel_id=1, replica_groups=mesh['seq'=32,'head'=8] {'seq'}, dimensions={0} | all-to-all | bytes 1966080 | tf_op jit(solution)/shard_map/all_to_all | solution.py:75
  197.2 5.7 %all-to-all-start.8 = ((bf16[32,40,384]{2,1,0:T(8,128)(2,1)}), bf16[32,40,384]{2,1,0:T(8,128)(2,1)}, u32[]{:S(2)}, u32[]{:S(2)}) async-start(bf16[32,40,384]{2,1,0:T(8,128)(2,1)} %get-tuple-element.69), calls=%async_computation.8 | async-start | bytes 1966080 | tf_op jit(solution)/shard_map/all_to_all | solution.py:75
  203.3 3.7 %concatenate.24 = bf16[1280,3,128]{2,1,0:T(4,128)(2,1)} reshape(bf16[8,160,384]{2,1,0:T(8,128)(2,1)} %bitcast.9) | data formatting | bytes 1966080 | tf_op jit(solution)/shard_map/concatenate | solution.py:88
  213.5 3.7 %concatenate.22 = bf16[1280,3,128]{2,1,0:T(4,128)(2,1)} reshape(bf16[32,40,384]{2,1,0:T(8,128)(2,1)} %all_to_all.99) | data formatting | bytes 1966080 | tf_op jit(solution)/shard_map/concatenate | solution.py:87
  217.2 26.4 %pad_maximum_fusion = bf16[3840,3,128]{2,1,0:T(4,128)(2,1)S(1)} fusion(bf16[1280,3,128]{2,1,0:T(4,128)(2,1)} %concatenate.22, bf16[1280,3,128]{2,1,0:T(4,128)(2,1)S(1)} %concatenate.21, bf16[1280,3,128]{2,1,0:T(4,128)(2,1)S(1)} %concatenate.20), kind=kLoop, calls=%fused_computation.21 | loop fusion | flops 2949120 | bytes 5898240 | tf_op jit(solution)/shard_map/concatenate | solution.py:87
  244.1 3.7 %concatenate.25 = bf16[1280,3,128]{2,1,0:T(4,128)(2,1)} reshape(bf16[32,40,384]{2,1,0:T(8,128)(2,1)} %all_to_all.100) | data formatting | bytes 1966080 | tf_op jit(solution)/shard_map/concatenate | solution.py:88
  247.8 3.7 %concatenate.26 = bf16[1280,3,128]{2,1,0:T(4,128)(2,1)} reshape(bf16[32,40,384]{2,1,0:T(8,128)(2,1)} %all-to-all-done.8) | data formatting | bytes 1966080 | tf_op jit(solution)/shard_map/concatenate | solution.py:88
  251.5 11.2 %pad_maximum_fusion.1 = bf16[3840,3,128]{2,1,0:T(4,128)(2,1)S(1)} fusion(bf16[1280,3,128]{2,1,0:T(4,128)(2,1)} %concatenate.26, bf16[1280,3,128]{2,1,0:T(4,128)(2,1)} %concatenate.25, bf16[1280,3,128]{2,1,0:T(4,128)(2,1)} %concatenate.24), kind=kLoop, calls=%fused_computation.22 | loop fusion | flops 2949120 | bytes 5898240 | tf_op jit(solution)/shard_map/concatenate | solution.py:88
  264.6 40.9 %while.10 = (s32[]{:T(128)}, bf16[5,256,3,128]{3,1,2,0:T(8,128)(2,1)}, bf16[5,256,3,128]{3,1,2,0:T(8,128)(2,1)}, bf16[3840,3,128]{2,0,1:T(8,128)(2,1)S(1)}, bf16[3840,3,128]{2,0,1:T(8,128)(2,1)}, /*index=5*/s32[]{:T(128)}) while((s32[]{:T(128)}, bf16[5,256,3,128]{3,1,2,0:T(8,128)(2,1)}, bf16[5,256,3,128]{3,1,2,0:T(8,128)(2,1)}, ...), condition=%wide.region_3.5_spmd, body=%wide.region_0.4_spmd.sunk | while | flops 1533737472 | bytes 53493856 | solution.py:36
  269.4 3.4 %fusion.37 = bf16[5,256,3,128]{3,1,2,0:T(8,128)(2,1)} fusion(bf16[5,256,3,128]{3,1,2,0:T(8,128)(2,1)} %get-tuple-element.113, s32[]{:T(128)} %get-tuple-element.112, bf16[3840,3,128]{2,0,1:T(8,128)(2,1)S(1)} %copy-done.1, f32[3,256,3840]{2,1,0:T(8,128)S(1)} %get-tuple-element.104, f32[3,256]{1,0:T(4,128)S(1)} %get-tuple-element.105, ...), kind=kOutput, calls=%fused_computation.15.clone.1 | convolution fusion | flops 764018688 | bytes 14948864 | tf_op jit(solution)/shard_map/while/body/eval_jaxpr/hqk,khd->qhd/dot_general | solution.py:28
  285.8 3.4 %fusion.37 = bf16[5,256,3,128]{3,1,2,0:T(8,128)(2,1)} fusion(bf16[5,256,3,128]{3,1,2,0:T(8,128)(2,1)} %get-tuple-element.113, s32[]{:T(128)} %get-tuple-element.112, bf16[3840,3,128]{2,0,1:T(8,128)(2,1)S(1)} %copy-done.1, f32[3,256,3840]{2,1,0:T(8,128)S(1)} %get-tuple-element.104, f32[3,256]{1,0:T(4,128)S(1)} %get-tuple-element.105, ...), kind=kOutput, calls=%fused_computation.15.clone.1 | convolution fusion | flops 764018688 | bytes 14948864 | tf_op jit(solution)/shard_map/while/body/eval_jaxpr/hqk,khd->qhd/dot_general | solution.py:28
  302.1 3.4 %fusion.37 = bf16[5,256,3,128]{3,1,2,0:T(8,128)(2,1)} fusion(bf16[5,256,3,128]{3,1,2,0:T(8,128)(2,1)} %get-tuple-element.113, s32[]{:T(128)} %get-tuple-element.112, bf16[3840,3,128]{2,0,1:T(8,128)(2,1)S(1)} %copy-done.1, f32[3,256,3840]{2,1,0:T(8,128)S(1)} %get-tuple-element.104, f32[3,256]{1,0:T(4,128)S(1)} %get-tuple-element.105, ...), kind=kOutput, calls=%fused_computation.15.clone.1 | convolution fusion | flops 764018688 | bytes 14948864 | tf_op jit(solution)/shard_map/while/body/eval_jaxpr/hqk,khd->qhd/dot_general | solution.py:28
  308.5 28.7 %all_to_all.101 = bf16[8,160,384]{2,1,0:T(8,128)(2,1)S(1)} all-to-all(bf16[8,160,384]{2,1,0:T(8,128)(2,1)S(1)} %all_to_all.83), channel_id=1, replica_groups=mesh['seq'=32,'head'=8] {'head'}, dimensions={0} | all-to-all | bytes 1966080 | tf_op jit(solution)/shard_map/all_to_all | solution.py:90
  (51 shorter events, 61.0 us)
Async XLA Ops:
  0.0 12.3 %copy-start.2 = (bf16[160,3072]{1,0:T(8,128)(2,1)S(1)}, bf16[160,3072]{1,0:T(8,128)(2,1)}, u32[]{:S(2)}) copy-start(bf16[160,3072]{1,0:T(8,128)(2,1)} %param.10) | copy-start | bytes 2949124
  2.3 33.0 %all-to-all-start.1 = ((bf16[160,8,384]{2,0,1:T(8,128)(2,1)}), bf16[160,8,384]{2,0,1:T(8,128)(2,1)S(1)}, u32[]{:S(2)}, u32[]{:S(2)}) async-start(bf16[160,8,384]{2,0,1:T(8,128)(2,1)} %bitcast.48), calls=%async_computation.1 | async-start | bytes 1966080 | tf_op jit(solution)/shard_map/all_to_all | solution.py:43
  67.7 48.0 %copy-start.3 = (s32[2,32]{1,0:T(2,128)S(1)}, s32[2,32]{1,0:T(2,128)}, u32[]{:S(2)}) copy-start(s32[2,32]{1,0:T(2,128)} %param.11) | copy-start | bytes 772
  89.2 16.8 %all-to-all-start.6 = ((bf16[32,40,384]{2,1,0:T(8,128)(2,1)}), bf16[32,40,384]{2,1,0:T(8,128)(2,1)S(1)}, u32[]{:S(2)}, u32[]{:S(2)}) async-start(bf16[32,40,384]{2,1,0:T(8,128)(2,1)} %bitcast.10), calls=%async_computation.6 | async-start | bytes 1966080 | tf_op jit(solution)/shard_map/all_to_all | solution.py:56
  106.0 30.3 %all-to-all-start = ((bf16[160,8,384]{2,0,1:T(8,128)(2,1)}), bf16[160,8,384]{2,0,1:T(8,128)(2,1)}, u32[]{:S(2)}, u32[]{:S(2)}) async-start(bf16[160,8,384]{2,0,1:T(8,128)(2,1)} %bitcast.64), calls=%async_computation | async-start | bytes 1966080 | tf_op jit(solution)/shard_map/all_to_all | solution.py:42
  136.3 25.3 %all-to-all-start.3 = ((bf16[32,40,384]{2,1,0:T(8,128)(2,1)}), bf16[32,40,384]{2,1,0:T(8,128)(2,1)}, u32[]{:S(2)}, u32[]{:S(2)}) async-start(bf16[32,40,384]{2,1,0:T(8,128)(2,1)} %get-tuple-element.68), calls=%async_computation.3 | async-start | bytes 1966080 | tf_op jit(solution)/shard_map/all_to_all | solution.py:68
  149.3 31.0 %copy-start = (bf16[32,40,384]{2,1,0:T(8,128)(2,1)S(1)}, bf16[32,40,384]{2,1,0:T(8,128)(2,1)}, u32[]{:S(2)}) copy-start(bf16[32,40,384]{2,1,0:T(8,128)(2,1)} %get-tuple-element.67) | copy-start | bytes 2949124
  197.2 50.5 %all-to-all-start.8 = ((bf16[32,40,384]{2,1,0:T(8,128)(2,1)}), bf16[32,40,384]{2,1,0:T(8,128)(2,1)}, u32[]{:S(2)}, u32[]{:S(2)}) async-start(bf16[32,40,384]{2,1,0:T(8,128)(2,1)} %get-tuple-element.69), calls=%async_computation.8 | async-start | bytes 1966080 | tf_op jit(solution)/shard_map/all_to_all | solution.py:75
  267.3 2.1 copy-start.1
  275.5 2.1 copy-start.1
  283.7 2.1 copy-start.1
  291.9 2.1 copy-start.1
  300.1 2.1 copy-start.1
where the time goes:
time: 345 us; the launch traced here: 338 us
  blocking collectives  118 us (34%)
  waiting for transfers between devices  54.2 us (16%)
  other arithmetic  53.7 us (16%)
  starting transfers between devices  42 us (12%)
  local copies, waits for them, and re-layouts  39.4 us (11%)
  matrix products  30.6 us (9%)
    all_to_all x1, blocking collectives, per_device(): lax.all_to_all(value_tokens, 'head', split_axis=1, concat_axis=0, tiled=T...  32.4 us
    all_to_all x1, blocking collectives, per_device(): lax.all_to_all(attended, 'head', split_axis=0, concat_axis=1, tiled=True)  28.7 us
    concatenate x1, other arithmetic, per_device(): key_rows = jnp.concatenate([local_keys, partner_keys], 0)  26.4 us
    all_to_all x1, waiting for transfers between devices, per_device(): lax.all_to_all(key_tokens, 'head', split_axis=1, concat_axis=0, tiled=True)  22.9 us
    all_to_all x1, blocking collectives, per_device(): lax.all_to_all(local_keys.reshape(seq_count, piece_rows, feature_width),...  21.4 us
    all_to_all x1, blocking collectives, per_device(): lax.all_to_all(jnp.take(spread_keys, matching[round_index], axis=0), 'seq...  18.8 us
    dot_general x5, matrix products, one_block(): jnp.einsum('hqk,khd->qhd', weights.astype(jnp.bfloat16), value_heads, pre...  17 us
    all_to_all x1, blocking collectives, per_device(): lax.all_to_all(jnp.take(spread_values, matching[round_index], axis=0), 's...  16.9 us
  transfers between devices with their start and end apart: 5, of which 4 were waited for; matrix products, arithmetic and copies ran while one was open for 18% of the time, Pallas kernels for 0%

commit v1 on v0

v1 whole, which is shorter than its diff:
```python
import math

import jax
import jax.numpy as jnp
from jax import lax
from jax.experimental import pallas as pl
from jax.experimental.pallas import tpu as pltpu
from jax.sharding import PartitionSpec as P

HEAD_DIM = 128
ROUNDS = 2
BLOCKS = 32
BLOCK_TOK = 1280
SHARD_TOK = 160
WIDTH = 3072
LEVELS = 8
SIDE = 4
PLANE = SIDE * SIDE
GROUP = WIDTH // HEAD_DIM // LEVELS
PIECE = BLOCK_TOK // PLANE
TILE = 256
EXP2_SCALE = math.log2(math.e) / math.sqrt(HEAD_DIM)
MESH = pl.DeviceIdType.MESH
KEY, VALUE, QUERY = range(3)


def rows(start, size, step=None):
    return pl.ds(pl.multiple_of(start, step or size), size)


def attend_chunk(query, keys, values, before=None):
    scores = lax.dot_general(query, keys, (((1,), (1,)), ((), ())), preferred_element_type=jnp.float32)
    largest = jnp.max(scores, axis=-1, keepdims=True)
    if before is not None:
        largest = jnp.maximum(largest, before[0])
    weights = jnp.exp2((scores - largest) * EXP2_SCALE)
    totals = jnp.sum(weights, axis=-1, keepdims=True)
    mixed = jnp.dot(weights.astype(jnp.bfloat16), values, preferred_element_type=jnp.float32)
    if before is not None:
        shrink = jnp.exp2((before[0] - largest) * EXP2_SCALE)
        totals += before[1] * shrink
        mixed += before[2] * shrink
    return largest, totals, mixed


def kernel(match_ref, query_ref, key_ref, value_ref, out_ref, *scratch):
    (shards, near, query, largest, totals, mixed, done) = scratch[:7]
    spread, stage, partner = scratch[7:10], scratch[10:13], scratch[13:16]
    load_sem, send_sem, near_sem, spread_send, spread_sem, partner_send, partner_sem, out_send, out_sem = scratch[16:]

    seq, head = lax.axis_index("seq"), lax.axis_index("head")
    z_low, chip = lax.div(seq, PLANE), lax.rem(seq, PLANE)
    z_high, core = lax.div(head, 2), lax.rem(head, 2)
    x, y = lax.div(chip, SIDE), lax.rem(chip, SIDE)
    level = z_high * 2 + z_low
    block = core * PLANE + chip

    def column_device(at_level, at_core):
        return lax.rem(at_level, 2) * PLANE + chip, lax.div(at_level, 2) * 2 + at_core

    def plane_device(at_chip, at_core):
        return z_low * PLANE + at_chip, z_high * 2 + at_core

    def plane_chip(step):
        across = lax.rem(step, SIDE)
        down = lax.rem(lax.div(step, SIDE) + across, SIDE)
        return lax.rem(x + across, SIDE) * SIDE + lax.rem(y + down, SIDE)

    def put(source, target, send, recv, device):
        here = jnp.logical_and(device[0] == seq, device[1] == head)

        @pl.when(here)
        def _():
            pltpu.make_async_copy(source, target, recv).start()

        @pl.when(jnp.logical_not(here))
        def _():
            pltpu.make_async_remote_copy(source, target, send, recv, device_id=device, device_id_type=MESH).start()

    def wait_bytes(ref, sem):
        pltpu.make_async_copy(ref, ref, sem).wait()

    for array, ref in ((KEY, key_ref), (VALUE, value_ref), (QUERY, query_ref)):
        pltpu.make_async_copy(ref, shards.at[array], load_sem.at[array]).start()

    barrier = pltpu.get_barrier_semaphore()

    def greet_column(step, carry):
        device = column_device(lax.rem(level + lax.div(step, 2), LEVELS), lax.rem(core + lax.rem(step, 2), 2))
        pl.semaphore_signal(barrier, inc=1, device_id=device, device_id_type=MESH)
        return carry

    def greet_plane(step, carry):
        device = plane_device(plane_chip(lax.div(step, 2)), lax.rem(step, 2))
        pl.semaphore_signal(barrier, inc=1, device_id=device, device_id_type=MESH)
        return carry

    lax.fori_loop(1, 2 * LEVELS, greet_column, 0)
    lax.fori_loop(2, 2 * PLANE, greet_plane, 0)
    pl.semaphore_wait(barrier, 2 * LEVELS + 2 * PLANE - 3)

    def near_target(array, index):
        return query.at[index] if array == QUERY else near.at[index, array]

    def send_near(index, array):
        def one(step, carry):
            sign = 1 - 2 * lax.rem(step, 2)
            to = lax.rem(level + LEVELS // 2 + sign * lax.div(step + 1, 2), LEVELS)
            put(
                shards.at[array, :, rows((to * GROUP + index) * HEAD_DIM, HEAD_DIM)],
                near_target(array, index).at[rows(head * SHARD_TOK, SHARD_TOK)],
                send_sem.at[index, array],
                near_sem.at[index, array],
                column_device(to, z_low),
            )
            return carry

        lax.fori_loop(0, LEVELS, one, 0)

    def wait_near(index, array):
        wait_bytes(near_target(array, index), near_sem.at[index, array])

    def send_spread(index, at_core):
        def one(step, carry):
            to = plane_chip(step)
            put(
                near.at[index, at_core, rows(to * PIECE, PIECE)],
                spread[index].at[block],
                spread_send.at[index],
                spread_sem.at[index],
                plane_device(to, at_core),
            )
            return carry

        lax.fori_loop(0, PLANE, one, 0)

    def send_partner(index):
        wait_bytes(spread[index], spread_sem.at[index])

        def one(step, carry):
            to, at_core = plane_chip(lax.div(step, 2)), lax.rem(step, 2)
            owner = at_core * PLANE + to
            for round_index in range(ROUNDS):
                stage[index][owner, round_index * PIECE : (round_index + 1) * PIECE, :] = spread[index][
                    match_ref[round_index, owner]
                ]
            put(
                stage[index].at[owner],
                partner[index].at[core, chip],
                partner_send.at[index],
                partner_sem.at[index],
                plane_device(to, at_core),
            )
            return carry

        lax.fori_loop(0, BLOCKS, one, 0)

    def attend_near(index):
        def one(step, carry):
            at = rows(step * TILE, TILE)
            found = attend_chunk(query[index, at], near[index, KEY], near[index, VALUE])
            largest[index, at], totals[index, at], mixed[index, at] = found
            return carry

        lax.fori_loop(0, BLOCK_TOK // TILE, one, 0)

    def attend_partner(index):
        wait_bytes(partner[index], partner_sem.at[index])
        keys = partner[index].at[KEY]
        values = partner[index].at[VALUE]

        def one(step, carry):
            at = rows(step * TILE, TILE)
            _, sums, found = attend_chunk(
                query[index, at],
                keys[...].reshape(ROUNDS * BLOCK_TOK, HEAD_DIM),
                values[...].reshape(ROUNDS * BLOCK_TOK, HEAD_DIM),
                (largest[index, at], totals[index, at], mixed[index, at]),
            )
            done[index, at] = (found / sums).astype(jnp.bfloat16)
            return carry

        lax.fori_loop(0, BLOCK_TOK // TILE, one, 0)

        def give(step, carry):
            to = lax.rem(head + step, LEVELS)
            put(
                done.at[index, rows(to * SHARD_TOK, SHARD_TOK)],
                out_ref.at[:, rows((level * GROUP + index) * HEAD_DIM, HEAD_DIM)],
                out_send.at[index],
                out_sem,
                (block, to),
            )
            return carry

        lax.fori_loop(0, LEVELS, give, 0)

    for array in (KEY, VALUE, QUERY):
        wait_bytes(shards.at[array], load_sem.at[array])
    for index in range(GROUP):
        for array in (KEY, VALUE, QUERY):
            send_near(index, array)

    def spread_both(index):
        for array in (KEY, VALUE):
            wait_near(index, array)
            send_spread(index, array)

    spread_both(0)
    wait_near(0, QUERY)
    attend_near(0)
    send_partner(0)
    spread_both(1)
    wait_near(1, QUERY)
    attend_near(1)
    send_partner(1)
    attend_partner(0)
    spread_both(2)
    send_partner(2)
    wait_near(2, QUERY)
    attend_near(2)
    attend_partner(1)
    attend_partner(2)

    own = core == z_low

    for index in range(GROUP):
        for array in (KEY, VALUE, QUERY):
            @pl.when(own)
            def _():
                wait_bytes(query.at[index, pl.ds(0, (LEVELS - 1) * SHARD_TOK)], send_sem.at[index, array])

            @pl.when(jnp.logical_not(own))
            def _():
                wait_bytes(query.at[index], send_sem.at[index, array])

        wait_bytes(spread[index].at[pl.ds(0, BLOCKS - 1)], spread_send.at[index])
        wait_bytes(stage[index].at[pl.ds(0, BLOCKS - 1)], partner_send.at[index])

        @pl.when(own)
        def _():
            wait_bytes(done.at[index, pl.ds(0, (LEVELS - 1) * SHARD_TOK)], out_send.at[index])

        @pl.when(jnp.logical_not(own))
        def _():
            wait_bytes(done.at[index], out_send.at[index])

    wait_bytes(out_ref, out_sem)


def per_device(query_tokens, key_tokens, value_tokens, matching):
    whole = pl.BlockSpec(memory_space=pl.ANY)
    bf16, f32 = jnp.bfloat16, jnp.float32
    return pl.pallas_call(
        kernel,
        out_shape=jax.ShapeDtypeStruct(query_tokens.shape, bf16),
        in_specs=[pl.BlockSpec(memory_space=pltpu.SMEM), whole, whole, whole],
        out_specs=whole,
        scratch_shapes=[
            pltpu.VMEM((3, SHARD_TOK, WIDTH), bf16),
            pltpu.VMEM((GROUP, 2, BLOCK_TOK, HEAD_DIM), bf16),
            pltpu.VMEM((GROUP, BLOCK_TOK, HEAD_DIM), bf16),
            pltpu.VMEM((GROUP, BLOCK_TOK, 1), f32),
            pltpu.VMEM((GROUP, BLOCK_TOK, 1), f32),
            pltpu.VMEM((GROUP, BLOCK_TOK, HEAD_DIM), f32),
            pltpu.VMEM((GROUP, BLOCK_TOK, HEAD_DIM), bf16),
            *[pltpu.VMEM((BLOCKS, PIECE, HEAD_DIM), bf16)] * GROUP,
            *[pltpu.VMEM((BLOCKS, ROUNDS * PIECE, HEAD_DIM), bf16)] * GROUP,
            *[pltpu.VMEM((2, PLANE, ROUNDS * PIECE, HEAD_DIM), bf16)] * GROUP,
            pltpu.SemaphoreType.DMA((3,)),
            pltpu.SemaphoreType.DMA((GROUP, 3)),
            pltpu.SemaphoreType.DMA((GROUP, 3)),
            pltpu.SemaphoreType.DMA((GROUP,)),
            pltpu.SemaphoreType.DMA((GROUP,)),
            pltpu.SemaphoreType.DMA((GROUP,)),
            pltpu.SemaphoreType.DMA((GROUP,)),
            pltpu.SemaphoreType.DMA((GROUP,)),
            pltpu.SemaphoreType.DMA,
        ],
        compiler_params=pltpu.CompilerParams(
            collective_id=0, has_side_effects=True, vmem_limit_bytes=56 * 2**20
        ),
    )(matching, query_tokens, key_tokens, value_tokens)


def solution(mesh):
    return jax.shard_map(
        per_device,
        mesh=mesh,
        in_specs=(
            P(("seq", "head"), None),
            P(("seq", "head"), None),
            P(("seq", "head"), None),
            P(),
        ),
        out_specs=P(("seq", "head"), None),
        check_vma=False,
    )
```

time: 345 us -> 126 us (0.37); the launches traced: 338 us -> 126 us
  Pallas kernels: 0 us -> 123 us
  blocking collectives: 118 us -> 0 us
  waiting for transfers between devices: 54.2 us -> 0 us
  other arithmetic: 53.7 us -> 0 us
  starting transfers between devices: 42 us -> 0 us
  local copies, waits for them, and re-layouts: 39.4 us -> 2.21 us
  matrix products: 30.6 us -> 0 us
    pallas_call x0 -> x1, Pallas kernels: none -> 123 us  [per_device(): pl.pallas_call(kernel, out_shape=jax.ShapeDtypeStruct(query_tokens.shape,...]
    all_to_all x5 -> x0, blocking collectives: 118 us -> none  [the longest x1 32.4 us: per_device(): lax.all_to_all(value_tokens, 'head', split_axis=1, concat_axis=0, tiled=T...]
    all_to_all x5 -> x0, waiting for transfers between devices: 54.2 us -> none  [the longest x1 22.9 us: per_device(): lax.all_to_all(key_tokens, 'head', split_axis=1, concat_axis=0, tiled=True)]
    all_to_all x5 -> x0, starting transfers between devices: 42 us -> none  [the longest x1 11.3 us: per_device(): lax.all_to_all(jnp.take(spread_keys, matching[round_index], axis=0), 'seq...]
    concatenate x2 -> x0, other arithmetic: 37.6 us -> none  [the longest x1 26.4 us: per_device(): key_rows = jnp.concatenate([local_keys, partner_keys], 0)]
    dot_general x10 -> x0, matrix products: 30.6 us -> none  [the longest x5 17 us: one_block(): jnp.einsum('hqk,khd->qhd', weights.astype(jnp.bfloat16), value_heads, pre...]
    concatenate x6 -> x0, local copies, waits for them, and re-layouts: 17.8 us -> none  [the longest x3 11.1 us: per_device(): value_rows = jnp.concatenate([local_values, partner_values], 0)]
    reduce_sum x5 -> x0, other arithmetic: 10.3 us -> none  [one_block(): totals = jnp.sum(weights, axis=-1)]
  transfers between devices with their start and end apart: 5 -> 0, of which waited for: 4 -> 0; matrix products, arithmetic and copies ran while one was open for 18% -> 0% of each run, Pallas kernels for 0% -> 0%
where the time goes in v1:
time: 126 us
  Pallas kernels  123 us (98%)
  local copies, waits for them, and re-layouts  2.21 us (2%)
    pallas_call x1, Pallas kernels, per_device(): pl.pallas_call(kernel, out_shape=jax.ShapeDtypeStruct(query_tokens.shape,...  123 us

profile of v1, /device:TPU:1, one launch (start us, length us, event | category | flops | bytes accessed | tf_op | source)
XLA Modules:
  0.0 125.5 jit_solution(1628935967033499249)
XLA Ops:
  0.0 123.3 %shard_map.46 = bf16[160,3072]{1,0:T(8,128)(2,1)} custom-call(s32[2,32]{1,0:T(2,128)} %match_ref.1, bf16[160,3072]{1,0:T(8,128)(2,1)} %query_ref.1, bf16[160,3072]{1,0:T(8,128)(2,1)} %key_ref.1, bf16[160,3072]{1,0:T(8,128)(2,1)} %value_ref.1), custom_call_target="tpu_custom_call" | custom-call | tf_op jit(solution)/shard_map/pallas_call | solution.py:254
  123.3 2.2 %copy.6 = bf16[160,3072]{1,0:T(8,128)(2,1)} copy(bf16[160,3072]{1,0:T(8,128)(2,1)} %shard_map.46) | data formatting | bytes 1966080

commit v2 on v1

--- a/solution.py
+++ b/solution.py
@@ -1,3 +1,4 @@
+import functools
 import math
 
 import jax
@@ -18,24 +19,42 @@
 PLANE = SIDE * SIDE
 GROUP = WIDTH // HEAD_DIM // LEVELS
 PIECE = BLOCK_TOK // PLANE
-TILE = 256
+CHUNK = 256
 EXP2_SCALE = math.log2(math.e) / math.sqrt(HEAD_DIM)
 MESH = pl.DeviceIdType.MESH
 KEY, VALUE, QUERY = range(3)
+NEAR_ORDER = (
+    (KEY, 0),
+    (VALUE, 0),
+    (QUERY, 0),
+    (KEY, 1),
+    (VALUE, 1),
+    (KEY, 2),
+    (VALUE, 2),
+    (QUERY, 1),
+    (QUERY, 2),
+)
+ROUND_SETS = (((0, 1),), ((0, 1),), ((0,), (1,)))
+PARTS = (1, 1, 2)
 
 
 def rows(start, size, step=None):
     return pl.ds(pl.multiple_of(start, step or size), size)
 
 
-def attend_chunk(query, keys, values, before=None):
-    scores = lax.dot_general(query, keys, (((1,), (1,)), ((), ())), preferred_element_type=jnp.float32)
-    largest = jnp.max(scores, axis=-1, keepdims=True)
+def attend_chunks(query, pairs, before=None):
+    scores = [
+        lax.dot_general(keys, query, (((1,), (1,)), ((), ())), preferred_element_type=jnp.float32)
+        for keys, _ in pairs
+    ]
+    largest = functools.reduce(jnp.maximum, [jnp.max(part, axis=0, keepdims=True) for part in scores])
     if before is not None:
         largest = jnp.maximum(largest, before[0])
-    weights = jnp.exp2((scores - largest) * EXP2_SCALE)
-    totals = jnp.sum(weights, axis=-1, keepdims=True)
-    mixed = jnp.dot(weights.astype(jnp.bfloat16), values, preferred_element_type=jnp.float32)
+    totals, mixed = 0.0, 0.0
+    for part, (_, values) in zip(scores, pairs):
+        weights = jnp.exp2((part - largest) * EXP2_SCALE)
+        totals += jnp.sum(weights, axis=0, keepdims=True)
+        mixed += jnp.dot(values, weights.astype(jnp.bfloat16), preferred_element_type=jnp.float32)
     if before is not None:
         shrink = jnp.exp2((before[0] - largest) * EXP2_SCALE)
         totals += before[1] * shrink
@@ -44,9 +63,9 @@
 
 
 def kernel(match_ref, query_ref, key_ref, value_ref, out_ref, *scratch):
-    (shards, near, query, largest, totals, mixed, done) = scratch[:7]
-    spread, stage, partner = scratch[7:10], scratch[10:13], scratch[13:16]
-    load_sem, send_sem, near_sem, spread_send, spread_sem, partner_send, partner_sem, out_send, out_sem = scratch[16:]
+    (shards, near, query, largest, totals, mixed, done, turned) = scratch[:8]
+    spread, stage, partner = scratch[8:11], scratch[11:14], scratch[14:17]
+    load_sem, send_sem, near_sem, spread_send, spread_sem, partner_send, partner_sem, out_send, out_sem = scratch[17:]
 
     seq, head = lax.axis_index("seq"), lax.axis_index("head")
     z_low, chip = lax.div(seq, PLANE), lax.rem(seq, PLANE)
@@ -136,54 +155,57 @@
 
     def send_partner(index):
         wait_bytes(spread[index], spread_sem.at[index])
-
-        def one(step, carry):
-            to, at_core = plane_chip(lax.div(step, 2)), lax.rem(step, 2)
-            owner = at_core * PLANE + to
-            for round_index in range(ROUNDS):
-                stage[index][owner, round_index * PIECE : (round_index + 1) * PIECE, :] = spread[index][
-                    match_ref[round_index, owner]
-                ]
-            put(
-                stage[index].at[owner],
-                partner[index].at[core, chip],
-                partner_send.at[index],
-                partner_sem.at[index],
-                plane_device(to, at_core),
-            )
-            return carry
-
-        lax.fori_loop(0, BLOCKS, one, 0)
+        for rounds in ROUND_SETS[index]:
+
+            def one(step, carry):
+                to, at_core = plane_chip(lax.div(step, 2)), lax.rem(step, 2)
+                owner = at_core * PLANE + to
+                for round_index in rounds:
+                    stage[index][round_index, owner] = spread[index][match_ref[round_index, owner]]
+                span = pl.ds(rounds[0], len(rounds))
+                put(
+                    stage[index].at[span, owner],
+                    partner[index].at[span, core, rows(chip * PIECE, PIECE)],
+                    partner_send.at[index, rounds[0]],
+                    partner_sem.at[index, rounds[0]],
+                    plane_device(to, at_core),
+                )
+                return carry
+
+            lax.fori_loop(0, BLOCKS, one, 0)
+
+    def chunks(ref, turned):
+        spans = [slice(start, start + CHUNK) for start in range(0, BLOCK_TOK, CHUNK)]
+        return [(ref[KEY, span], turned[:, span]) for span in spans]
+
+    def keep(index, found):
+        largest[index], totals[index], mixed[index] = found
 
     def attend_near(index):
-        def one(step, carry):
-            at = rows(step * TILE, TILE)
-            found = attend_chunk(query[index, at], near[index, KEY], near[index, VALUE])
-            largest[index, at], totals[index, at], mixed[index, at] = found
-            return carry
-
-        lax.fori_loop(0, BLOCK_TOK // TILE, one, 0)
-
-    def attend_partner(index):
-        wait_bytes(partner[index], partner_sem.at[index])
-        keys = partner[index].at[KEY]
-        values = partner[index].at[VALUE]
-
-        def one(step, carry):
-            at = rows(step * TILE, TILE)
-            _, sums, found = attend_chunk(
-                query[index, at],
-                keys[...].reshape(ROUNDS * BLOCK_TOK, HEAD_DIM),
-                values[...].reshape(ROUNDS * BLOCK_TOK, HEAD_DIM),
-                (largest[index, at], totals[index, at], mixed[index, at]),
-            )
-            done[index, at] = (found / sums).astype(jnp.bfloat16)
-            return carry
-
-        lax.fori_loop(0, BLOCK_TOK // TILE, one, 0)
-
-        def give(step, carry):
-            to = lax.rem(head + step, LEVELS)
+        turned[0] = near[index, VALUE].T
+        keep(index, attend_chunks(query[index], chunks(near.at[index], turned.at[0])))
+
+    def attend_partner(index, rounds):
+        wait_bytes(partner[index].at[pl.ds(rounds[0], len(rounds))], partner_sem.at[index, rounds[0]])
+        pairs = []
+        for round_index in rounds:
+            turned[round_index] = partner[index][round_index, VALUE].T
+            pairs += chunks(partner[index].at[round_index], turned.at[round_index])
+        last = rounds[-1] == ROUNDS - 1
+        parts = PARTS[index] if last else 1
+        width = BLOCK_TOK // parts
+        for part in range(parts):
+            at = slice(part * width, (part + 1) * width)
+            before = largest[index, :, at], totals[index, :, at], mixed[index, :, at]
+            found = attend_chunks(query[index, at], pairs, before)
+            if not last:
+                keep(index, found)
+                continue
+            done[index, at] = (found[2] / found[1]).T.astype(jnp.bfloat16)
+            give(index, part * LEVELS // parts, (part + 1) * LEVELS // parts)
+
+    def give(index, first, end):
+        def one(to, carry):
             put(
                 done.at[index, rows(to * SHARD_TOK, SHARD_TOK)],
                 out_ref.at[:, rows((level * GROUP + index) * HEAD_DIM, HEAD_DIM)],
@@ -193,34 +215,37 @@
             )
             return carry
 
-        lax.fori_loop(0, LEVELS, give, 0)
+        lax.fori_loop(first, end, one, 0)
 
     for array in (KEY, VALUE, QUERY):
         wait_bytes(shards.at[array], load_sem.at[array])
-    for index in range(GROUP):
-        for array in (KEY, VALUE, QUERY):
-            send_near(index, array)
-
-    def spread_both(index):
-        for array in (KEY, VALUE):
-            wait_near(index, array)
-            send_spread(index, array)
-
-    spread_both(0)
-    wait_near(0, QUERY)
-    attend_near(0)
+    for array, index in NEAR_ORDER:
+        send_near(index, array)
+
+    def spread_one(index, array):
+        wait_near(index, array)
+        send_spread(index, array)
+
+    def near_part(index):
+        wait_near(index, QUERY)
+        attend_near(index)
+
+    spread_one(0, KEY)
+    spread_one(0, VALUE)
     send_partner(0)
-    spread_both(1)
-    wait_near(1, QUERY)
-    attend_near(1)
+    near_part(0)
+    spread_one(1, KEY)
+    spread_one(1, VALUE)
     send_partner(1)
-    attend_partner(0)
-    spread_both(2)
+    attend_partner(0, (0, 1))
+    spread_one(2, KEY)
+    spread_one(2, VALUE)
+    near_part(1)
     send_partner(2)
-    wait_near(2, QUERY)
-    attend_near(2)
-    attend_partner(1)
-    attend_partner(2)
+    attend_partner(1, (0, 1))
+    near_part(2)
+    attend_partner(2, (0,))
+    attend_partner(2, (1,))
 
     own = core == z_low
 
@@ -235,7 +260,8 @@
                 wait_bytes(query.at[index], send_sem.at[index, array])
 
         wait_bytes(spread[index].at[pl.ds(0, BLOCKS - 1)], spread_send.at[index])
-        wait_bytes(stage[index].at[pl.ds(0, BLOCKS - 1)], partner_send.at[index])
+        for rounds in ROUND_SETS[index]:
+            wait_bytes(stage[index].at[pl.ds(rounds[0], len(rounds)), pl.ds(0, BLOCKS - 1)], partner_send.at[index, rounds[0]])
 
         @pl.when(own)
         def _():
@@ -260,20 +286,21 @@
             pltpu.VMEM((3, SHARD_TOK, WIDTH), bf16),
             pltpu.VMEM((GROUP, 2, BLOCK_TOK, HEAD_DIM), bf16),
             pltpu.VMEM((GROUP, BLOCK_TOK, HEAD_DIM), bf16),
-            pltpu.VMEM((GROUP, BLOCK_TOK, 1), f32),
-            pltpu.VMEM((GROUP, BLOCK_TOK, 1), f32),
-            pltpu.VMEM((GROUP, BLOCK_TOK, HEAD_DIM), f32),
+            pltpu.VMEM((GROUP, 1, BLOCK_TOK), f32),
+            pltpu.VMEM((GROUP, 1, BLOCK_TOK), f32),
+            pltpu.VMEM((GROUP, HEAD_DIM, BLOCK_TOK), f32),
             pltpu.VMEM((GROUP, BLOCK_TOK, HEAD_DIM), bf16),
+            pltpu.VMEM((ROUNDS, HEAD_DIM, BLOCK_TOK), bf16),
             *[pltpu.VMEM((BLOCKS, PIECE, HEAD_DIM), bf16)] * GROUP,
-            *[pltpu.VMEM((BLOCKS, ROUNDS * PIECE, HEAD_DIM), bf16)] * GROUP,
-            *[pltpu.VMEM((2, PLANE, ROUNDS * PIECE, HEAD_DIM), bf16)] * GROUP,
+            *[pltpu.VMEM((ROUNDS, BLOCKS, PIECE, HEAD_DIM), bf16)] * GROUP,
+            *[pltpu.VMEM((ROUNDS, 2, BLOCK_TOK, HEAD_DIM), bf16)] * GROUP,
             pltpu.SemaphoreType.DMA((3,)),
             pltpu.SemaphoreType.DMA((GROUP, 3)),
             pltpu.SemaphoreType.DMA((GROUP, 3)),
             pltpu.SemaphoreType.DMA((GROUP,)),
             pltpu.SemaphoreType.DMA((GROUP,)),
-            pltpu.SemaphoreType.DMA((GROUP,)),
-            pltpu.SemaphoreType.DMA((GROUP,)),
+            pltpu.SemaphoreType.DMA((GROUP, ROUNDS)),
+            pltpu.SemaphoreType.DMA((GROUP, ROUNDS)),
             pltpu.SemaphoreType.DMA((GROUP,)),
             pltpu.SemaphoreType.DMA,
         ],

time: 126 us -> 110 us (0.87)
  Pallas kernels: 123 us -> 108 us
    pallas_call x1, Pallas kernels: 123 us -> 108 us  [per_device(): pl.pallas_call(kernel, out_shape=jax.ShapeDtypeStruct(query_tokens.shape,...]
where the time goes in v2:
time: 110 us
  Pallas kernels  108 us (98%)
  local copies, waits for them, and re-layouts  2.21 us (2%)
    pallas_call x1, Pallas kernels, per_device(): pl.pallas_call(kernel, out_shape=jax.ShapeDtypeStruct(query_tokens.shape,...  108 us
    unnamed x1, local copies, waits for them, and re-layouts  2.21 us

profile of v2, /device:TPU:1, one launch (start us, length us, event | category | flops | bytes accessed | tf_op | source)
XLA Modules:
  0.0 110.3 jit_solution(5023482107522740775)
XLA Ops:
  0.0 108.0 %shard_map.46 = bf16[160,3072]{1,0:T(8,128)(2,1)} custom-call(s32[2,32]{1,0:T(2,128)} %match_ref.1, bf16[160,3072]{1,0:T(8,128)(2,1)} %query_ref.1, bf16[160,3072]{1,0:T(8,128)(2,1)} %key_ref.1, bf16[160,3072]{1,0:T(8,128)(2,1)} %value_ref.1), custom_call_target="tpu_custom_call" | custom-call | tf_op jit(solution)/shard_map/pallas_call | solution.py:280
  108.1 2.2 %copy.6 = bf16[160,3072]{1,0:T(8,128)(2,1)} copy(bf16[160,3072]{1,0:T(8,128)(2,1)} %shard_map.46) | data formatting | bytes 1966080

commit v3 on v2

--- a/solution.py
+++ b/solution.py
@@ -23,17 +23,6 @@
 EXP2_SCALE = math.log2(math.e) / math.sqrt(HEAD_DIM)
 MESH = pl.DeviceIdType.MESH
 KEY, VALUE, QUERY = range(3)
-NEAR_ORDER = (
-    (KEY, 0),
-    (VALUE, 0),
-    (QUERY, 0),
-    (KEY, 1),
-    (VALUE, 1),
-    (KEY, 2),
-    (VALUE, 2),
-    (QUERY, 1),
-    (QUERY, 2),
-)
 ROUND_SETS = (((0, 1),), ((0, 1),), ((0,), (1,)))
 PARTS = (1, 1, 2)
 
@@ -65,7 +54,7 @@
 def kernel(match_ref, query_ref, key_ref, value_ref, out_ref, *scratch):
     (shards, near, query, largest, totals, mixed, done, turned) = scratch[:8]
     spread, stage, partner = scratch[8:11], scratch[11:14], scratch[14:17]
-    load_sem, send_sem, near_sem, spread_send, spread_sem, partner_send, partner_sem, out_send, out_sem = scratch[17:]
+    load_sem, send_sem, near_sem, spread_send, spread_sem, partner_send, partner_sem, out_send, out_sem, line_sem, core_sem = scratch[17:]
 
     seq, head = lax.axis_index("seq"), lax.axis_index("head")
     z_low, chip = lax.div(seq, PLANE), lax.rem(seq, PLANE)
@@ -81,8 +70,8 @@
         return z_low * PLANE + at_chip, z_high * 2 + at_core
 
     def plane_chip(step):
-        across = lax.rem(step, SIDE)
-        down = lax.rem(lax.div(step, SIDE) + across, SIDE)
+        across = lax.rem(lax.div(step, SIDE) + step, SIDE)
+        down = lax.rem(step * 3 + lax.div(step, SIDE) * 2, SIDE)
         return lax.rem(x + across, SIDE) * SIDE + lax.rem(y + down, SIDE)
 
     def put(source, target, send, recv, device):
@@ -109,14 +98,19 @@
         pl.semaphore_signal(barrier, inc=1, device_id=device, device_id_type=MESH)
         return carry
 
-    def greet_plane(step, carry):
-        device = plane_device(plane_chip(lax.div(step, 2)), lax.rem(step, 2))
-        pl.semaphore_signal(barrier, inc=1, device_id=device, device_id_type=MESH)
-        return carry
-
     lax.fori_loop(1, 2 * LEVELS, greet_column, 0)
-    lax.fori_loop(2, 2 * PLANE, greet_plane, 0)
-    pl.semaphore_wait(barrier, 2 * LEVELS + 2 * PLANE - 3)
+    for step in range(1, SIDE):
+        for at_chip in (lax.rem(x + step, SIDE) * SIDE + y, x * SIDE + lax.rem(y + step, SIDE)):
+            pl.semaphore_signal(barrier, inc=1, device_id=plane_device(at_chip, core), device_id_type=MESH)
+    pl.semaphore_wait(barrier, 2 * LEVELS - 1 + 2 * (SIDE - 1))
+
+    def greet_plane():
+        for step in range(1, SIDE):
+            at_chip = x * SIDE + lax.rem(y + step, SIDE)
+            pl.semaphore_signal(line_sem, inc=1, device_id=plane_device(at_chip, core), device_id_type=MESH)
+        pl.semaphore_wait(line_sem, SIDE - 1)
+        pl.semaphore_signal(core_sem, inc=1, device_id=(seq, z_high * 2 + 1 - core), device_id_type=MESH)
+        pl.semaphore_wait(core_sem, 1)
 
     def near_target(array, index):
         return query.at[index] if array == QUERY else near.at[index, array]
@@ -158,7 +152,7 @@
         for rounds in ROUND_SETS[index]:
 
             def one(step, carry):
-                to, at_core = plane_chip(lax.div(step, 2)), lax.rem(step, 2)
+                to, at_core = plane_chip(lax.rem(step, PLANE)), lax.div(step, PLANE)
                 owner = at_core * PLANE + to
                 for round_index in rounds:
                     stage[index][round_index, owner] = spread[index][match_ref[round_index, owner]]
@@ -219,31 +213,37 @@
 
     for array in (KEY, VALUE, QUERY):
         wait_bytes(shards.at[array], load_sem.at[array])
-    for array, index in NEAR_ORDER:
-        send_near(index, array)
-
     def spread_one(index, array):
         wait_near(index, array)
         send_spread(index, array)
 
-    def near_part(index):
-        wait_near(index, QUERY)
-        attend_near(index)
-
+    send_near(0, KEY)
+    send_near(0, VALUE)
+    send_near(0, QUERY)
+    greet_plane()
     spread_one(0, KEY)
+    send_near(1, KEY)
     spread_one(0, VALUE)
+    send_near(1, VALUE)
     send_partner(0)
-    near_part(0)
+    wait_near(0, QUERY)
+    send_near(2, KEY)
+    attend_near(0)
     spread_one(1, KEY)
+    send_near(2, VALUE)
     spread_one(1, VALUE)
+    send_near(1, QUERY)
     send_partner(1)
     attend_partner(0, (0, 1))
     spread_one(2, KEY)
+    send_near(2, QUERY)
     spread_one(2, VALUE)
-    near_part(1)
+    wait_near(1, QUERY)
+    attend_near(1)
     send_partner(2)
     attend_partner(1, (0, 1))
-    near_part(2)
+    wait_near(2, QUERY)
+    attend_near(2)
     attend_partner(2, (0,))
     attend_partner(2, (1,))
 
@@ -303,6 +303,8 @@
             pltpu.SemaphoreType.DMA((GROUP, ROUNDS)),
             pltpu.SemaphoreType.DMA((GROUP,)),
             pltpu.SemaphoreType.DMA,
+            pltpu.SemaphoreType.REGULAR,
+            pltpu.SemaphoreType.REGULAR,
         ],
         compiler_params=pltpu.CompilerParams(
             collective_id=0, has_side_effects=True, vmem_limit_bytes=56 * 2**20

time: 110 us -> 106 us (0.964)
  Pallas kernels: 108 us -> 103 us
    pallas_call x1, Pallas kernels: 108 us -> 103 us  [per_device(): pl.pallas_call(kernel, out_shape=jax.ShapeDtypeStruct(query_tokens.shape,...]
where the time goes in v3:
time: 106 us
  Pallas kernels  103 us (97%)
  local copies, waits for them, and re-layouts  2.21 us (2%)
    pallas_call x1, Pallas kernels, per_device(): pl.pallas_call(kernel, out_shape=jax.ShapeDtypeStruct(query_tokens.shape,...  103 us
    unnamed x1, local copies, waits for them, and re-layouts  2.21 us

profile of v3, /device:TPU:1, one launch (start us, length us, event | category | flops | bytes accessed | tf_op | source)
XLA Modules:
  0.0 105.6 jit_solution(2864739907518342080)
XLA Ops:
  0.0 103.3 %shard_map.46 = bf16[160,3072]{1,0:T(8,128)(2,1)} custom-call(s32[2,32]{1,0:T(2,128)} %match_ref.1, bf16[160,3072]{1,0:T(8,128)(2,1)} %query_ref.1, bf16[160,3072]{1,0:T(8,128)(2,1)} %key_ref.1, bf16[160,3072]{1,0:T(8,128)(2,1)} %value_ref.1), custom_call_target="tpu_custom_call" | custom-call | tf_op jit(solution)/shard_map/pallas_call | solution.py:280
  103.3 2.2 %copy.6 = bf16[160,3072]{1,0:T(8,128)(2,1)} copy(bf16[160,3072]{1,0:T(8,128)(2,1)} %shard_map.46) | data formatting | bytes 1966080

commit v4 on v3

--- a/solution.py
+++ b/solution.py
@@ -307,7 +307,7 @@
             pltpu.SemaphoreType.REGULAR,
         ],
         compiler_params=pltpu.CompilerParams(
-            collective_id=0, has_side_effects=True, vmem_limit_bytes=56 * 2**20
+            collective_id=0, has_side_effects=True, vmem_limit_bytes=48 * 2**20
         ),
     )(matching, query_tokens, key_tokens, value_tokens)
 

time: 106 us -> 110 us (1.038)
  local copies, waits for them, and re-layouts: 2.21 us -> 5.23 us
    unnamed x1 -> x9, local copies, waits for them, and re-layouts: 2.21 us -> 5.23 us
where the time goes in v4:
time: 110 us; the launch traced here: 109 us
  Pallas kernels  104 us (95%)
  local copies, waits for them, and re-layouts  5.23 us (5%)
    pallas_call x1, Pallas kernels, per_device(): pl.pallas_call(kernel, out_shape=jax.ShapeDtypeStruct(query_tokens.shape,...  104 us
    unnamed x9, local copies, waits for them, and re-layouts  5.23 us

profile of v4, /device:TPU:1, one launch (start us, length us, event | category | flops | bytes accessed | tf_op | source)
XLA Modules:
  0.0 109.5 jit_solution(8317589674202922666)
XLA Ops:
  0.0 0.0 copy-start
  0.0 1.2 %copy-done = bf16[160,3072]{1,0:T(8,128)(2,1)S(1)} copy-done((bf16[160,3072]{1,0:T(8,128)(2,1)S(1)}, bf16[160,3072]{1,0:T(8,128)(2,1)}, u32[]{:S(2)}) %copy-start) | copy-done | bytes 983064
  1.2 0.0 copy-start.1
  1.2 1.2 %copy-done.1 = bf16[160,3072]{1,0:T(8,128)(2,1)S(1)} copy-done((bf16[160,3072]{1,0:T(8,128)(2,1)S(1)}, bf16[160,3072]{1,0:T(8,128)(2,1)}, u32[]{:S(2)}) %copy-start.1) | copy-done | bytes 983064
  2.4 0.0 copy-start.2
  2.4 1.2 %copy-done.2 = bf16[160,3072]{1,0:T(8,128)(2,1)S(1)} copy-done((bf16[160,3072]{1,0:T(8,128)(2,1)S(1)}, bf16[160,3072]{1,0:T(8,128)(2,1)}, u32[]{:S(2)}) %copy-start.2) | copy-done | bytes 983064
  3.6 0.0 copy-start.3
  3.6 0.7 copy-done.3
  4.3 104.3 %shard_map.46 = bf16[160,3072]{1,0:T(8,128)(2,1)S(1)} custom-call(s32[2,32]{1,0:T(2,128)S(1)} %copy-done.3, bf16[160,3072]{1,0:T(8,128)(2,1)S(1)} %copy-done, bf16[160,3072]{1,0:T(8,128)(2,1)S(1)} %copy-done.1, bf16[160,3072]{1,0:T(8,128)(2,1)S(1)} %copy-done.2), custom_call_target="tpu_custom_call" | custom-call | tf_op jit(solution)/shard_map/pallas_call | solution.py:280
  108.6 0.9 copy.6
Async XLA Ops:
  0.0 1.2 %copy-start = (bf16[160,3072]{1,0:T(8,128)(2,1)S(1)}, bf16[160,3072]{1,0:T(8,128)(2,1)}, u32[]{:S(2)}) copy-start(bf16[160,3072]{1,0:T(8,128)(2,1)} %query_ref.1) | copy-start | bytes 2949124
  1.2 1.2 %copy-start.1 = (bf16[160,3072]{1,0:T(8,128)(2,1)S(1)}, bf16[160,3072]{1,0:T(8,128)(2,1)}, u32[]{:S(2)}) copy-start(bf16[160,3072]{1,0:T(8,128)(2,1)} %key_ref.1) | copy-start | bytes 2949124
  2.4 1.2 %copy-start.2 = (bf16[160,3072]{1,0:T(8,128)(2,1)S(1)}, bf16[160,3072]{1,0:T(8,128)(2,1)}, u32[]{:S(2)}) copy-start(bf16[160,3072]{1,0:T(8,128)(2,1)} %value_ref.1) | copy-start | bytes 2949124
  3.6 0.7 copy-start.3
